TPU v7x, 32 devices: a whole 2x2x4 slice. The times are simulated.
32 devices in a mesh: section: 8 (over y, x, core), expert: 4 (over z).
Axes of the slice: x: 2, y: 2, z: 4, core: 2. Of those that a mesh axis runs over, the one named last changes fastest.
Arguments:
- tokens: bfloat16 [16384, 2880], P(('section', 'expert')), may hold values from -6 to 6
- segment_norm_scale: float32 [8, 2880], P('section'), may hold values from 0.1 to 1.9
- expert_choice_table: int32 [4, 16384, 4], P(None, ('section', 'expert')), may hold values from 0 to 127, as said below
- router_weight_table: bfloat16 [4, 16384, 4], P(None, ('section', 'expert')), may hold values from 0.099609375 to 1
- adapter_down_weight: bfloat16 [8, 2880, 128], P('section'), may hold values from -0.109375 to 0.109375
- adapter_up_weight: bfloat16 [8, 128, 2880], P('section'), may hold values from -0.5 to 0.5
- expert_gate_up_weight: bfloat16 [8, 2880, 2, 1440], P('section', None, None, 'expert'), may hold values from -0.109375 to 0.109375
- expert_down_weight: bfloat16 [8, 1440, 2880], P('section', 'expert'), may hold values from -0.15625 to 0.15625
Outputs:
- carried: bfloat16 [16384, 2880], P(('section', 'expert'))
Inputs may be any that keep to these rules, and one draw needn't show every extreme that they name: `expert_choice_table`: each row names 4 different experts. Within the rows of one device at one hop, at most 48 rows name expert 0, and in each hop some device has exactly 48 such rows.
All inputs are finite; a program needn't handle non-finite values.
Results may differ from a plain program's by a relative error of at most 0.014.
Values may be sent and summed in bfloat16 or wider, within the bound.
A program may use at most 128 MiB of HBM per device.

v0:
```python
import jax
import jax.numpy as jnp
from jax import lax
from jax.sharding import PartitionSpec as P

CAP = 48


def passed_along(value, axis, steps):
    count = lax.axis_size(axis)
    pairs = [(source, (source + steps) % count) for source in range(count)]
    return lax.ppermute(value, axis, pairs)


def window_slots(expert_choice_rows, slots):
    flags = jnp.any(expert_choice_rows == 0, axis=-1)
    flag_int = flags.astype(jnp.int32)
    position = jnp.cumsum(flag_int) - flag_int
    return jnp.where(flags, position, slots)


def selection(slot_index, slots):
    return (jnp.arange(slots, dtype=jnp.int32)[:, None] == slot_index[None, :]).astype(jnp.bfloat16)


def window_share(expert_choice_rows, mix_row):
    mix_values = mix_row.astype(jnp.float32)
    chosen = jnp.sum(jnp.where(expert_choice_rows == 0, mix_values, 0.0), axis=-1)
    return chosen / jnp.sum(mix_values, axis=-1)


def settle(adapted_values, slot_index, share, expert_out):
    slots = expert_out.shape[0]
    inside = slot_index < slots
    fetched = jnp.take(expert_out, jnp.minimum(slot_index, slots - 1), axis=0)
    picked = jnp.where(inside[:, None], fetched, 0.0)
    return (adapted_values + share[:, None] * picked).astype(jnp.bfloat16)


def body(
    tokens,
    segment_norm_scale,
    expert_choice_table,
    router_weight_table,
    adapter_down_weight,
    adapter_up_weight,
    expert_gate_up_weight,
    expert_down_weight,
):
    tok_rows, width = tokens.shape
    hid_dev = expert_down_weight.shape[1]
    gain_row = segment_norm_scale[0]
    adapter_down_factor = adapter_down_weight[0]
    adapter_up_factor = adapter_up_weight[0]
    weight_in = expert_gate_up_weight[0].reshape(width, 2 * hid_dev)
    weight_out = expert_down_weight[0]
    travelling_state = tokens
    for hop_index in range(expert_choice_table.shape[0]):
        values = travelling_state.astype(jnp.float32)
        scale = lax.rsqrt(jnp.mean(values * values, axis=-1, keepdims=True) + 1e-05)
        normed = (values * scale * gain_row).astype(jnp.bfloat16)
        low = jnp.dot(normed, adapter_down_factor, preferred_element_type=jnp.float32).astype(
            jnp.bfloat16
        )
        adapted = (
            values + jnp.dot(low, adapter_up_factor, preferred_element_type=jnp.float32)
        ).astype(jnp.bfloat16)
        expert_choice_rows = expert_choice_table[hop_index]
        slot_index = window_slots(expert_choice_rows, CAP)
        select = selection(slot_index, CAP)
        share = window_share(expert_choice_rows, router_weight_table[hop_index])
        slot_rows = jnp.dot(select, normed, preferred_element_type=jnp.float32).astype(jnp.bfloat16)
        joined = jnp.dot(
            lax.all_gather(slot_rows, "expert", axis=0, tiled=True),
            weight_in,
            preferred_element_type=jnp.float32,
        )
        gate_part = joined[:, :hid_dev]
        up_part = joined[:, hid_dev:]
        activated = (gate_part * jax.nn.sigmoid(1.702 * gate_part) * (up_part + 1.0)).astype(
            jnp.bfloat16
        )
        expert_out = lax.psum_scatter(
            jnp.dot(activated, weight_out, preferred_element_type=jnp.float32).astype(jnp.bfloat16),
            "expert",
            scatter_dimension=0,
            tiled=True,
        ).astype(jnp.float32)
        updated = settle(adapted.astype(jnp.float32), slot_index, share, expert_out)
        travelling_state = passed_along(updated, "section", 1)
    return travelling_state


def solution(mesh):
    return jax.shard_map(
        body,
        mesh=mesh,
        in_specs=(
            P(("section", "expert"), None),
            P("section", None),
            P(None, ("section", "expert"), None),
            P(None, ("section", "expert"), None),
            P("section", None, None),
            P("section", None, None),
            P("section", None, None, "expert"),
            P("section", "expert", None),
        ),
        out_specs=P(("section", "expert"), None),
        check_vma=False,
    )
```

profile of v0, /device:TPU:24, one launch (start us, length us, event | category | flops | bytes accessed | tf_op | source)
XLA Modules:
  0.0 518.7 jit_solution(5719399111007847182)
XLA Ops:
  6.5 0.9 fusion.99
  7.5 0.8 convert_reduce_fusion
  8.3 0.3 reduce-window.34
  8.6 0.1 slice.78
  8.7 0.1 slice_reduce_fusion.3
  8.8 0.1 broadcast_compare_fusion.3
  8.9 2.5 fusion
  11.5 0.7 reduce.12
  12.2 3.6 convolution_convert_fusion.7
  15.9 28.9 %all-gather.5.cloned.1.call-done = bf16[192,2880]{1,0:T(8,128)(2,1)} async-done(((bf16[48,2880]{1,0:T(8,128)(2,1)}), bf16[192,2880]{1,0:T(8,128)(2,1)}) %all-gather.5.cloned.1.call-update) | async-done | bytes 1105936 | tf_op jit(solution)/shard_map/all_gather | solution.py:74
  44.8 4.0 fusion.103
  48.8 1.8 convolution_convert_fusion.3
  50.8 27.3 %reduce-scatter.5.cloned.1.call-done = bf16[48,2880]{1,0:T(8,128)(2,1)} async-done(((bf16[192,2880]{1,0:T(8,128)(2,1)}), bf16[48,2880]{1,0:T(8,128)(2,1)}) %reduce-scatter.5.cloned.1.call-update) | async-done | bytes 276496 | tf_op jit(solution)/shard_map/reduce_scatter | solution.py:83
  78.1 1.0 convert_element_type.220
  79.1 4.6 gather_fusion
  83.7 6.5 %copy.13 = f32[512,2880]{0,1:T(8,128)} copy(f32[512,2880]{1,0:T(8,128)} %gather_fusion) | data formatting | bytes 11796480 | tf_op jit(solution)/shard_map/jit(_take)/gather | solution.py:35
  90.2 9.6 %fusion.27 = bf16[512,2880]{0,1:T(8,128)(2,1)} fusion(f32[512,2880]{0,1:T(8,128)} %copy.13, bf16[512,2880]{0,1:T(8,128)(2,1)} %param.10, f32[512]{0:T(512)S(1)} %div.53, pred[512]{0:T(512)(128)(4,1)S(1)} %compare_and_fusion.3, pred[512]{0:T(512)(128)(4,1)S(1)} %get-tuple-element.26, f32[2880]{0:T(1024)S(1)} %reduce.12, f32[512]{0:T(512)S(1)} %add_rsqrt_fusion.3, ...), kind=kOutput, calls=%fused_computation.47 | convolution fusion | flops 774209536 | bytes 13287680 | tf_op jit(solution)/shard_map/dot_general | solution.py:66
  99.8 0.3 reduce-window.36
  100.2 0.1 slice_reduce_fusion.2
  100.3 0.1 broadcast_compare_fusion.2
  100.4 35.2 %collective-permute-done = bf16[512,2880]{0,1:T(8,128)(2,1)} collective-permute-done((bf16[512,2880]{0,1:T(8,128)(2,1)}, bf16[512,2880]{0,1:T(8,128)(2,1)}, u32[]{:S(2)}, u32[]{:S(2)}) %collective-permute-start) | collective-permute-done | bytes 2949152 | tf_op jit(solution)/shard_map/ppermute | solution.py:12
  135.6 2.5 fusion.4
  138.1 3.6 convolution_convert_fusion.6
  141.8 0.2 reduce-scatter.7.cloned.1.call-start
  142.0 27.8 %all-gather.7.cloned.1.call-done = bf16[192,2880]{1,0:T(8,128)(2,1)} async-done(((bf16[48,2880]{1,0:T(8,128)(2,1)}), bf16[192,2880]{1,0:T(8,128)(2,1)}) %all-gather.7.cloned.1.call-update) | async-done | bytes 1105936 | tf_op jit(solution)/shard_map/all_gather | solution.py:74
  169.8 4.0 fusion.104
  173.8 1.8 convolution_convert_fusion.2
  175.8 27.3 %reduce-scatter.7.cloned.1.call-done = bf16[48,2880]{1,0:T(8,128)(2,1)} async-done(((bf16[192,2880]{1,0:T(8,128)(2,1)}), bf16[48,2880]{1,0:T(8,128)(2,1)}) %reduce-scatter.7.cloned.1.call-update) | async-done | bytes 276496 | tf_op jit(solution)/shard_map/reduce_scatter | solution.py:83
  203.1 1.0 convert_element_type.234
  204.1 4.6 gather_fusion.1
  208.7 6.5 %copy.14 = f32[512,2880]{0,1:T(8,128)} copy(f32[512,2880]{1,0:T(8,128)} %gather_fusion.1) | data formatting | bytes 11796480 | tf_op jit(solution)/shard_map/jit(_take)/gather | solution.py:35
  215.1 9.6 %fusion.24 = bf16[512,2880]{0,1:T(8,128)(2,1)} fusion(f32[512,2880]{0,1:T(8,128)} %copy.14, bf16[512,2880]{0,1:T(8,128)(2,1)} %collective-permute-done, f32[512]{0:T(512)S(1)} %div.56, pred[512]{0:T(512)(128)(4,1)S(1)} %compare_and_fusion.2, pred[512]{0:T(512)(128)(4,1)S(1)} %get-tuple-element.22, f32[512]{0:T(512)S(1)} %add_rsqrt_fusion.2, ...), kind=kOutput, calls=%fused_computation.43 | convolution fusion | flops 774209536 | bytes 13287680 | tf_op jit(solution)/shard_map/dot_general | solution.py:66
  224.7 0.3 reduce-window.48
  225.1 0.1 slice_reduce_fusion.1
  225.3 0.1 broadcast_compare_fusion.1
  225.3 35.2 %collective-permute-done.1 = bf16[512,2880]{0,1:T(8,128)(2,1)} collective-permute-done((bf16[512,2880]{0,1:T(8,128)(2,1)}, bf16[512,2880]{0,1:T(8,128)(2,1)}, u32[]{:S(2)}, u32[]{:S(2)}) %collective-permute-start.1) | collective-permute-done | bytes 2949152 | tf_op jit(solution)/shard_map/ppermute | solution.py:12
  260.5 2.5 fusion.8
  263.0 3.6 convolution_convert_fusion.5
  266.8 28.0 %all-gather.9.cloned.1.call-done = bf16[192,2880]{1,0:T(8,128)(2,1)} async-done(((bf16[48,2880]{1,0:T(8,128)(2,1)}), bf16[192,2880]{1,0:T(8,128)(2,1)}) %all-gather.9.cloned.1.call-update) | async-done | bytes 1105936 | tf_op jit(solution)/shard_map/all_gather | solution.py:74
  294.8 4.0 fusion.105
  298.7 1.8 convolution_convert_fusion.1
  300.6 0.3 all-gather.11.cloned.1.call-start
  300.9 27.1 %reduce-scatter.9.cloned.1.call-done = bf16[48,2880]{1,0:T(8,128)(2,1)} async-done(((bf16[192,2880]{1,0:T(8,128)(2,1)}), bf16[48,2880]{1,0:T(8,128)(2,1)}) %reduce-scatter.9.cloned.1.call-update) | async-done | bytes 276496 | tf_op jit(solution)/shard_map/reduce_scatter | solution.py:83
  328.0 1.0 convert_element_type.248
  329.0 4.6 gather_fusion.2
  333.6 6.5 %copy.15 = f32[512,2880]{0,1:T(8,128)} copy(f32[512,2880]{1,0:T(8,128)} %gather_fusion.2) | data formatting | bytes 11796480 | tf_op jit(solution)/shard_map/jit(_take)/gather | solution.py:35
  340.0 9.6 %fusion.21 = bf16[512,2880]{0,1:T(8,128)(2,1)} fusion(f32[512,2880]{0,1:T(8,128)} %copy.15, bf16[512,2880]{0,1:T(8,128)(2,1)} %collective-permute-done.1, f32[512]{0:T(512)S(1)} %div.59, pred[512]{0:T(512)(128)(4,1)S(1)} %compare_and_fusion.1, pred[512]{0:T(512)(128)(4,1)S(1)} %get-tuple-element.18, f32[512]{0:T(512)S(1)} %add_rsqrt_fusion.1, ...), kind=kOutput, calls=%fused_computation.39 | convolution fusion | flops 774209536 | bytes 13287680 | tf_op jit(solution)/shard_map/dot_general | solution.py:66
  349.6 0.3 reduce-window.50
  350.0 0.1 slice_reduce_fusion
  350.2 0.1 broadcast_compare_fusion
  350.2 35.2 %collective-permute-done.2 = bf16[512,2880]{0,1:T(8,128)(2,1)} collective-permute-done((bf16[512,2880]{0,1:T(8,128)(2,1)}, bf16[512,2880]{0,1:T(8,128)(2,1)}, u32[]{:S(2)}, u32[]{:S(2)}) %collective-permute-start.2) | collective-permute-done | bytes 2949152 | tf_op jit(solution)/shard_map/ppermute | solution.py:12
  385.4 2.5 fusion.12
  388.0 3.6 convolution_convert_fusion.4
  391.6 0.3 reduce-scatter.11.cloned.1.call-start
  391.9 27.7 %all-gather.11.cloned.1.call-done = bf16[192,2880]{1,0:T(8,128)(2,1)} async-done(((bf16[48,2880]{1,0:T(8,128)(2,1)}), bf16[192,2880]{1,0:T(8,128)(2,1)}) %all-gather.11.cloned.1.call-update) | async-done | bytes 1105936 | tf_op jit(solution)/shard_map/all_gather | solution.py:74
  419.7 4.0 fusion.106
  423.7 1.8 convolution_convert_fusion
  425.6 27.4 %reduce-scatter.11.cloned.1.call-done = bf16[48,2880]{1,0:T(8,128)(2,1)} async-done(((bf16[192,2880]{1,0:T(8,128)(2,1)}), bf16[48,2880]{1,0:T(8,128)(2,1)}) %reduce-scatter.11.cloned.1.call-update) | async-done | bytes 276496 | tf_op jit(solution)/shard_map/reduce_scatter | solution.py:83
  452.9 1.0 convert_element_type.262
  453.9 4.6 gather_fusion.3
  458.5 6.5 %copy.16 = f32[512,2880]{0,1:T(8,128)} copy(f32[512,2880]{1,0:T(8,128)} %gather_fusion.3) | data formatting | bytes 11796480 | tf_op jit(solution)/shard_map/jit(_take)/gather | solution.py:35
  464.9 9.6 %fusion.18 = bf16[512,2880]{0,1:T(8,128)(2,1)} fusion(f32[512,2880]{0,1:T(8,128)} %copy.16, bf16[512,2880]{0,1:T(8,128)(2,1)} %collective-permute-done.2, f32[512]{0:T(512)S(1)} %div.62, pred[512]{0:T(512)(128)(4,1)S(1)} %compare_and_fusion, pred[512]{0:T(512)(128)(4,1)S(1)} %get-tuple-element.14, f32[512]{0:T(512)S(1)} %add_rsqrt_fusion, ...), kind=kOutput, calls=%fused_computation.35 | convolution fusion | flops 774209536 | bytes 13287680 | tf_op jit(solution)/shard_map/dot_general | solution.py:66
  474.5 35.7 %collective-permute-done.3 = bf16[512,2880]{0,1:T(8,128)(2,1)S(1)} collective-permute-done((bf16[512,2880]{0,1:T(8,128)(2,1)}, bf16[512,2880]{0,1:T(8,128)(2,1)S(1)}, u32[]{:S(2)}, u32[]{:S(2)}) %collective-permute-start.3) | collective-permute-done | bytes 2949152 | tf_op jit(solution)/shard_map/ppermute | solution.py:12
  510.2 1.6 copy.18
  (52 shorter events, 0.8 us)
Async XLA Ops:
  6.5 42.3 %copy-start = (bf16[1,360,2880]{2,1,0:T(8,128)(2,1)S(1)}, bf16[1,360,2880]{2,1,0:T(8,128)(2,1)}, u32[]{:S(2)}) copy-start(bf16[1,360,2880]{2,1,0:T(8,128)(2,1)} %param.17) | copy-start | bytes 6220804
  6.5 38.3 %all-gather.5.cloned.1.call-start = ((), (), s32[]{:S(2)}) async-start(), calls=%async_computation.4 | async-start | bytes 1413120 | tf_op jit(solution)/shard_map/all_gather | solution.py:74
  15.9 62.2 %reduce-scatter.5.cloned.1.call-start = ((), (), s32[]{:S(2)}) async-start(), calls=%async_computation.5 | async-start | bytes 1413120 | tf_op jit(solution)/shard_map/reduce_scatter | solution.py:83
  50.7 119.1 %all-gather.7.cloned.1.call-start = ((), (), s32[]{:S(2)}) async-start(), calls=%async_computation.6 | async-start | bytes 1413120 | tf_op jit(solution)/shard_map/all_gather | solution.py:74
  83.7 6.5 %copy-start.1 = (bf16[1,128,2880]{1,2,0:T(8,128)(2,1)S(1)}, bf16[1,128,2880]{1,2,0:T(8,128)(2,1)}, u32[]{:S(2)}) copy-start(bf16[1,128,2880]{1,2,0:T(8,128)(2,1)} %param.15) | copy-start | bytes 2211844
  99.8 35.8 %collective-permute-start = (bf16[512,2880]{0,1:T(8,128)(2,1)}, bf16[512,2880]{0,1:T(8,128)(2,1)}, u32[]{:S(2)}, u32[]{:S(2)}) collective-permute-start(bf16[512,2880]{0,1:T(8,128)(2,1)} %fusion.27), channel_id=1, source_target_pairs={{0,4},{4,8},{8,12},{12,16},{16,20},{20,24},{24,28},{28,0},{1,5},{5... | collective-permute-start | bytes 8847368 | tf_op jit(solution)/shard_map/ppermute | solution.py:12
  141.8 61.3 %reduce-scatter.7.cloned.1.call-start = ((), (), s32[]{:S(2)}) async-start(), calls=%async_computation.7 | async-start | bytes 1413120 | tf_op jit(solution)/shard_map/reduce_scatter | solution.py:83
  175.7 119.1 %all-gather.9.cloned.1.call-start = ((), (), s32[]{:S(2)}) async-start(), calls=%async_computation.8 | async-start | bytes 1413120 | tf_op jit(solution)/shard_map/all_gather | solution.py:74
  224.7 35.8 %collective-permute-start.1 = (bf16[512,2880]{0,1:T(8,128)(2,1)}, bf16[512,2880]{0,1:T(8,128)(2,1)}, u32[]{:S(2)}, u32[]{:S(2)}) collective-permute-start(bf16[512,2880]{0,1:T(8,128)(2,1)} %fusion.24), channel_id=1, source_target_pairs={{0,4},{4,8},{8,12},{12,16},{16,20},{20,24},{24,28},{28,0},{1,5},{5... | collective-permute-start | bytes 8847368 | tf_op jit(solution)/shard_map/ppermute | solution.py:12
  266.7 61.3 %reduce-scatter.9.cloned.1.call-start = ((), (), s32[]{:S(2)}) async-start(), calls=%async_computation.9 | async-start | bytes 1413120 | tf_op jit(solution)/shard_map/reduce_scatter | solution.py:83
  300.6 119.1 %all-gather.11.cloned.1.call-start = ((), (), s32[]{:S(2)}) async-start(), calls=%async_computation.10 | async-start | bytes 1413120 | tf_op jit(solution)/shard_map/all_gather | solution.py:74
  349.6 35.8 %collective-permute-start.2 = (bf16[512,2880]{0,1:T(8,128)(2,1)}, bf16[512,2880]{0,1:T(8,128)(2,1)}, u32[]{:S(2)}, u32[]{:S(2)}) collective-permute-start(bf16[512,2880]{0,1:T(8,128)(2,1)} %fusion.21), channel_id=1, source_target_pairs={{0,4},{4,8},{8,12},{12,16},{16,20},{20,24},{24,28},{28,0},{1,5},{5... | collective-permute-start | bytes 8847368 | tf_op jit(solution)/shard_map/ppermute | solution.py:12
  391.6 61.3 %reduce-scatter.11.cloned.1.call-start = ((), (), s32[]{:S(2)}) async-start(), calls=%async_computation.11 | async-start | bytes 1413120 | tf_op jit(solution)/shard_map/reduce_scatter | solution.py:83
  474.5 35.7 %collective-permute-start.3 = (bf16[512,2880]{0,1:T(8,128)(2,1)}, bf16[512,2880]{0,1:T(8,128)(2,1)S(1)}, u32[]{:S(2)}, u32[]{:S(2)}) collective-permute-start(bf16[512,2880]{0,1:T(8,128)(2,1)} %fusion.18), channel_id=1, source_target_pairs={{0,4},{4,8},{8,12},{12,16},{16,20},{20,24},{24,28},{28,0},{1,5},{5... | collective-permute-start | bytes 8847368 | tf_op jit(solution)/shard_map/ppermute | solution.py:12
Sparse Core Ops, SparseCore 0:
  16.0 28.8 all-gather.4
  50.8 27.2 reduce-scatter.4
  141.9 27.8 all-gather.6
  175.8 27.2 reduce-scatter.6
  266.8 27.8 all-gather.8
  300.7 27.2 reduce-scatter.8
  391.8 27.8 all-gather.10
  425.6 27.2 reduce-scatter.10
where the time goes:
time: 524 us; the launch traced here: 519 us
  waiting for transfers between devices  363 us (69%)
  matrix products  76.3 us (15%)
  local copies, waits for them, and re-layouts  46.5 us (9%)
  other arithmetic  18.4 us (4%)
  between operations  13.7 us (3%)
    ppermute x4, waiting for transfers between devices, passed_along(): return lax.ppermute(value, axis, pairs)  141 us
    all_gather x4, waiting for transfers between devices, body(): lax.all_gather(slot_rows, 'expert', axis=0, tiled=True)  112 us
    reduce_scatter x4, waiting for transfers between devices, body(): lax.psum_scatter(jnp.dot(activated, weight_out, preferred_element_type=jn...  109 us
    gather x8, local copies, waits for them, and re-layouts, settle(): fetched = jnp.take(expert_out, jnp.minimum(slot_index, slots - 1), axis=0)  44.1 us
    dot_general x4, matrix products, body(): jnp.dot(low, adapter_up_factor, preferred_element_type=jnp.float32)  38.4 us
    dot_general x4, matrix products, body(): jnp.dot(lax.all_gather(slot_rows, 'expert', axis=0, tiled=True), weight_i...  15.9 us
    dot_general x4, matrix products, body(): jnp.dot(select, normed, preferred_element_type=jnp.float32)  14.6 us
  transfers between devices with their start and end apart: 12, of which 12 were waited for; matrix products, arithmetic and copies ran while one was open for 0% of the time, Pallas kernels for 0%

commit v1 on v0

v1 whole, which is shorter than its diff:
```python
import functools

import jax
import jax.numpy as jnp
from jax import lax
from jax.experimental import pallas as pl
from jax.experimental.pallas import tpu as pltpu
from jax.sharding import PartitionSpec as P

CAP = 48
LEFT, RIGHT = 0, 1


def row_tile(width):
    for tile in (320, 192, 64, 16):
        if width % tile == 0:
            return tile
    return width


def relay_kernel(
    n_section,
    n_expert,
    tokens_ref,
    gain_ref,
    choice_ref,
    router_ref,
    down_ref,
    up_ref,
    weight_in_ref,
    weight_out_ref,
    x_ref,
    normed,
    adapted,
    arrived,
    gain_col,
    square_sum,
    own_rows,
    gathered,
    partials,
    returned,
    expert_sum,
    expert_own,
    expert_in,
    meta_own,
    meta_in,
    down_v,
    up_v,
    weight_in_v,
    weight_out_v,
    load_sem,
    ag_send,
    ag_recv,
    rs_send,
    rs_recv,
    x_send,
    x_recv,
    e_send,
    e_recv,
    m_send,
    m_recv,
):
    section = lax.axis_index("section")
    expert = lax.axis_index("expert")
    hops = choice_ref.shape[0]
    width, rows = x_ref.shape
    tile = row_tile(width)
    steps = n_expert - 1
    following = lax.rem(section + 1, n_section)
    previous = lax.rem(section + n_section - 1, n_section)

    def place(to_section, to_expert):
        return {"section": to_section, "expert": to_expert}

    loads = [
        pltpu.make_async_copy(source, target, load_sem.at[i])
        for i, (source, target) in enumerate(
            (
                (tokens_ref, x_ref),
                (down_ref, down_v),
                (up_ref, up_v),
                (weight_in_ref, weight_in_v),
                (weight_out_ref, weight_out_v),
            )
        )
    ]
    for load in loads:
        load.start()

    barrier = pltpu.get_barrier_semaphore()
    for target in (
        place(following, expert),
        place(previous, expert),
        place(section, lax.rem(expert + 1, n_expert)),
        place(section, lax.rem(expert + n_expert - 1, n_expert)),
        place(section, lax.rem(expert + 2, n_expert)),
    ):
        pl.semaphore_signal(barrier, inc=1, device_id=target, device_id_type=pl.DeviceIdType.MESH)

    before = (
        lax.broadcasted_iota(jnp.int32, (rows, rows), 0)
        < lax.broadcasted_iota(jnp.int32, (rows, rows), 1)
    ).astype(jnp.float32).astype(jnp.bfloat16)
    meta_own[...] = jnp.zeros_like(meta_own)
    for hop in range(hops):
        picks = choice_ref[hop]
        mix = router_ref[hop].astype(jnp.float32)
        here = (picks == 0).astype(jnp.float32)
        flag = jnp.max(here, axis=0, keepdims=True)
        position = jnp.dot(
            jnp.broadcast_to(flag, (16, rows)).astype(jnp.bfloat16),
            before,
            preferred_element_type=jnp.float32,
        )[:1]
        chosen = jnp.sum(here * mix, axis=0, keepdims=True)
        total = jnp.sum(mix, axis=0, keepdims=True)
        meta_own[hop, 0:1, :] = jnp.where(flag > 0.0, position, float(CAP))
        meta_own[hop, 1:2, :] = chosen / total

    for start in range(0, width, 128):
        stop = min(start + 128, width)
        piece = jnp.broadcast_to(gain_ref[0:1, start:stop], (128, stop - start))
        gain_col[start:stop, :] = piece.T

    pl.semaphore_wait(barrier, 5)

    def remote(source, target, send, recv, device):
        return pltpu.make_async_remote_copy(
            src_ref=source,
            dst_ref=target,
            send_sem=send,
            recv_sem=recv,
            device_id=device,
            device_id_type=pl.DeviceIdType.MESH,
        )

    meta_copy = remote(meta_own, meta_in, m_send, m_recv, place(following, expert))
    meta_copy.start()

    def tiles(body):
        def step(i, carry):
            body(pl.ds(pl.multiple_of(i * tile, tile), tile))
            return carry

        lax.fori_loop(0, width // tile, step, 0)

    def add_squares(values):
        square_sum[...] += jnp.sum((values * values).reshape(tile // 8, 8, rows), axis=0)

    loads[0].wait()
    square_sum[...] = jnp.zeros_like(square_sum)

    def first_squares(at):
        add_squares(x_ref[at, :].astype(jnp.float32))

    tiles(first_squares)

    def one_hot(meta, hop):
        slots = lax.broadcasted_iota(jnp.int32, (CAP, rows), 0).astype(jnp.float32)
        return jnp.where(slots == meta[hop, 0:1, :], 1.0, 0.0).astype(jnp.bfloat16)

    def expert_partial(block):
        gate = lax.dot_general(
            block, weight_in_v[0], (((1,), (1,)), ((), ())), preferred_element_type=jnp.float32
        )
        up = lax.dot_general(
            block, weight_in_v[1], (((1,), (1,)), ((), ())), preferred_element_type=jnp.float32
        )
        activated = (gate * jax.nn.sigmoid(1.702 * gate) * (up + 1.0)).astype(jnp.bfloat16)
        return jnp.dot(
            activated, weight_out_v[...], preferred_element_type=jnp.float32
        ).astype(jnp.bfloat16)

    def left_at(distance):
        return expert >= distance

    def right_at(distance):
        return expert + distance < n_expert

    def gather_send(hop, k, side):
        source = own_rows.at[hop] if k == 0 else gathered.at[hop, k - 1, side]
        step = 1 if side == LEFT else -1
        return remote(
            source,
            gathered.at[hop, k, side],
            ag_send.at[hop, k, side],
            ag_recv.at[hop, k, side],
            place(section, lax.rem(expert + step + n_expert, n_expert)),
        )

    def gather_sends(hop, k):
        return (
            (left_at(k) & right_at(1), gather_send(hop, k, LEFT)),
            (right_at(k) & left_at(1), gather_send(hop, k, RIGHT)),
        )

    def partial_send(hop, k, side):
        away = -(k + 1) if side == LEFT else k + 1
        return remote(
            partials.at[k, side],
            returned.at[hop, k, 1 - side],
            rs_send.at[hop, k, side],
            rs_recv.at[hop, k, 1 - side],
            place(section, lax.rem(expert + away + n_expert, n_expert)),
        )

    def on_side(side, distance):
        return left_at(distance) if side == LEFT else right_at(distance)

    def hop_body(hop, carry):
        scale = lax.rsqrt(
            jnp.sum(square_sum[...], axis=0, keepdims=True) * (1.0 / width) + 1e-05
        )

        def normalise(at):
            gain = jnp.concatenate([gain_col[at, :]] * (rows // 128), axis=1)
            normed[at, :] = (x_ref[at, :].astype(jnp.float32) * scale * gain).astype(jnp.bfloat16)

        tiles(normalise)
        own_rows[hop] = lax.dot_general(
            one_hot(meta_own, hop),
            normed[...],
            (((1,), (1,)), ((), ())),
            preferred_element_type=jnp.float32,
        ).astype(jnp.bfloat16)
        for valid, copy in gather_sends(hop, 0):
            pl.when(valid)(copy.start)

        @pl.when(hop == 0)
        def _():
            loads[1].wait()
            loads[2].wait()

        low = lax.dot_general(
            down_v[...], normed[...], (((0,), (0,)), ((), ())), preferred_element_type=jnp.float32
        ).astype(jnp.bfloat16)

        def adapt(at):
            adapted[at, :] = (
                x_ref[at, :].astype(jnp.float32)
                + jnp.dot(up_v[at, :], low, preferred_element_type=jnp.float32)
            ).astype(jnp.bfloat16)

        tiles(adapt)
        stream_copy = remote(
            adapted, arrived.at[hop], x_send.at[hop], x_recv.at[hop], place(following, expert)
        )
        stream_copy.start()

        def take_and_forward(k):
            for side in (LEFT, RIGHT):
                pl.when(on_side(side, k + 1))(gather_send(hop, k, side).wait_recv)
            if k + 1 < steps:
                for valid, copy in gather_sends(hop, k + 1):
                    pl.when(valid)(copy.start)

        take_and_forward(0)

        @pl.when(hop == 0)
        def _():
            loads[3].wait()
            loads[4].wait()

        expert_sum[...] = expert_partial(own_rows[hop]).astype(jnp.float32)
        for k in range(steps):

            @pl.when(left_at(k + 1) | right_at(k + 1))
            def _(k=k):
                block = gathered[hop, k].reshape(2 * CAP, width)
                partials[k] = expert_partial(block).reshape(2, CAP, width)

            for side in (LEFT, RIGHT):
                pl.when(on_side(side, k + 1))(partial_send(hop, k, side).start)
            if k + 1 < steps:
                take_and_forward(k + 1)

        for k in range(steps):
            for side in (LEFT, RIGHT):

                @pl.when(on_side(side, k + 1))
                def _(k=k, side=side):
                    partial_send(hop, k, 1 - side).wait_recv()
                    expert_sum[...] += returned[hop, k, side].astype(jnp.float32)

        expert_own[hop] = expert_sum[...].astype(jnp.bfloat16)
        expert_copy = remote(
            expert_own.at[hop],
            expert_in.at[hop],
            e_send.at[hop],
            e_recv.at[hop],
            place(following, expert),
        )
        expert_copy.start()

        for k in range(steps):
            for valid, copy in gather_sends(hop, k):
                pl.when(valid)(copy.wait_send)
            for side in (LEFT, RIGHT):
                pl.when(on_side(side, k + 1))(partial_send(hop, k, side).wait_send)

        @pl.when(hop == 0)
        def _():
            meta_copy.wait()

        stream_copy.wait()
        expert_copy.wait()
        spread = one_hot(meta_in, hop)
        share = meta_in[hop, 1:2, :]
        square_sum[...] = jnp.zeros_like(square_sum)
        lanes = 384
        for start in range(0, width, lanes):
            stop = min(start + lanes, width)
            picked = lax.dot_general(
                expert_in[hop, :, start:stop],
                spread,
                (((0,), (0,)), ((), ())),
                preferred_element_type=jnp.float32,
            )
            moved = (
                arrived[hop, start:stop, :].astype(jnp.float32) + share * picked
            ).astype(jnp.bfloat16)
            x_ref[start:stop, :] = moved
            values = moved.astype(jnp.float32)
            square_sum[...] += jnp.sum(
                (values * values).reshape((stop - start) // 8, 8, rows), axis=0
            )
        return carry

    lax.fori_loop(0, hops, hop_body, 0)


def body(
    n_section,
    n_expert,
    tokens,
    segment_norm_scale,
    expert_choice_table,
    router_weight_table,
    adapter_down_weight,
    adapter_up_weight,
    expert_gate_up_weight,
    expert_down_weight,
):
    rows, width = tokens.shape
    hops, _, top = expert_choice_table.shape
    rank = adapter_down_weight.shape[2]
    hid = expert_down_weight.shape[1]
    steps = n_expert - 1
    half = jnp.bfloat16
    full = jnp.float32
    block = (CAP, width)
    dma = pltpu.SemaphoreType.DMA
    flops = hops * (4 * rows * width * rank + 6 * n_expert * CAP * width * hid)
    out = pl.pallas_call(
        functools.partial(relay_kernel, n_section, n_expert),
        out_shape=jax.ShapeDtypeStruct((width, rows), half),
        in_specs=[
            pl.BlockSpec(memory_space=pl.ANY),
            pl.BlockSpec(memory_space=pltpu.VMEM),
            pl.BlockSpec(memory_space=pltpu.VMEM),
            pl.BlockSpec(memory_space=pltpu.VMEM),
            pl.BlockSpec(memory_space=pl.ANY),
            pl.BlockSpec(memory_space=pl.ANY),
            pl.BlockSpec(memory_space=pl.ANY),
            pl.BlockSpec(memory_space=pl.ANY),
        ],
        out_specs=pl.BlockSpec(memory_space=pltpu.VMEM),
        scratch_shapes=[
            pltpu.VMEM((width, rows), half),
            pltpu.VMEM((width, rows), half),
            pltpu.VMEM((hops, width, rows), half),
            pltpu.VMEM((width, 128), full),
            pltpu.VMEM((8, rows), full),
            pltpu.VMEM((hops,) + block, half),
            pltpu.VMEM((hops, steps, 2) + block, half),
            pltpu.VMEM((steps, 2) + block, half),
            pltpu.VMEM((hops, steps, 2) + block, half),
            pltpu.VMEM(block, full),
            pltpu.VMEM((hops,) + block, half),
            pltpu.VMEM((hops,) + block, half),
            pltpu.VMEM((hops, 8, rows), full),
            pltpu.VMEM((hops, 8, rows), full),
            pltpu.VMEM((width, rank), half),
            pltpu.VMEM((width, rank), half),
            pltpu.VMEM((2, hid, width), half),
            pltpu.VMEM((hid, width), half),
            dma((5,)),
            dma((hops, steps, 2)),
            dma((hops, steps, 2)),
            dma((hops, steps, 2)),
            dma((hops, steps, 2)),
            dma((hops,)),
            dma((hops,)),
            dma((hops,)),
            dma((hops,)),
            dma,
            dma,
        ],
        compiler_params=pltpu.CompilerParams(
            collective_id=0, has_side_effects=True, vmem_limit_bytes=60 * 2**20
        ),
        cost_estimate=pl.CostEstimate(
            flops=flops, bytes_accessed=16 * 2**20, transcendentals=hops * n_expert * CAP * hid
        ),
    )(
        tokens.T,
        segment_norm_scale,
        jnp.transpose(expert_choice_table, (0, 2, 1)),
        jnp.transpose(router_weight_table, (0, 2, 1)),
        adapter_down_weight[0],
        adapter_up_weight[0].T,
        jnp.transpose(expert_gate_up_weight[0], (1, 2, 0)),
        expert_down_weight[0],
    )
    return out.T


def solution(mesh):
    return jax.shard_map(
        functools.partial(body, mesh.shape["section"], mesh.shape["expert"]),
        mesh=mesh,
        in_specs=(
            P(("section", "expert"), None),
            P("section", None),
            P(None, ("section", "expert"), None),
            P(None, ("section", "expert"), None),
            P("section", None, None),
            P("section", None, None),
            P("section", None, None, "expert"),
            P("section", "expert", None),
        ),
        out_specs=P(("section", "expert"), None),
        check_vma=False,
    )
```

time: 524 us -> 220 us (0.42)
  waiting for transfers between devices: 363 us -> 0 us
  Pallas kernels: 0 us -> 216 us
  matrix products: 76.3 us -> 0 us
  local copies, waits for them, and re-layouts: 46.5 us -> 3.62 us
  other arithmetic: 18.4 us -> 0 us
  between operations: 13.7 us -> 0.01 us
    pallas_call x0 -> x1, Pallas kernels: none -> 216 us  [body(): pl.pallas_call(functools.partial(relay_kernel, n_section, n_expert), out_...]
    ppermute x4 -> x0, waiting for transfers between devices: 141 us -> none  [passed_along(): return lax.ppermute(value, axis, pairs)]
    all_gather x4 -> x0, waiting for transfers between devices: 112 us -> none  [body(): lax.all_gather(slot_rows, 'expert', axis=0, tiled=True)]
    reduce_scatter x4 -> x0, waiting for transfers between devices: 109 us -> none  [body(): lax.psum_scatter(jnp.dot(activated, weight_out, preferred_element_type=jn...]
    dot_general x16 -> x0, matrix products: 76.3 us -> none  [the longest x4 38.4 us: body(): jnp.dot(low, adapter_up_factor, preferred_element_type=jnp.float32)]
    gather x8 -> x0, local copies, waits for them, and re-layouts: 44.1 us -> none  [settle(): fetched = jnp.take(expert_out, jnp.minimum(slot_index, slots - 1), axis=0)]
    reduce_sum x5 -> x0, other arithmetic: 10.9 us -> none  [the longest x4 10.1 us: body(): scale = lax.rsqrt(jnp.mean(values * values, axis=-1, keepdims=True) + 1e-05)]
  transfers between devices with their start and end apart: 12 -> 0, of which waited for: 12 -> 0; matrix products, arithmetic and copies ran while one was open for 0% -> 0% of each run, Pallas kernels for 0% -> 0%
where the time goes in v1:
time: 220 us
  Pallas kernels  216 us (98%)
  local copies, waits for them, and re-layouts  3.62 us (2%)
    pallas_call x1, Pallas kernels, body(): pl.pallas_call(functools.partial(relay_kernel, n_section, n_expert), out_...  216 us

profile of v1, /device:TPU:24, one launch (start us, length us, event | category | flops | bytes accessed | tf_op | source)
XLA Modules:
  0.0 219.8 jit_solution(7351753446846357629)
XLA Ops:
  0.0 216.2 %shard_map.82 = bf16[2880,512]{1,0:T(8,128)(2,1)} custom-call(bf16[2880,512]{1,0:T(8,128)(2,1)} %bitcast.14, f32[1,2880]{1,0:T(1,128)} %gain_ref.1, s32[4,4,512]{2,1,0:T(4,128)} %bitcast.18, bf16[4,4,512]{2,1,0:T(4,128)(2,1)} %bitcast.19, bf16[2880,128]{1,0:T(8,128)(2,1)} %bitcast.16, bf16[2880,128]{1,0:T(8,128)(2,1)} %bitcast.17, ...), custom_call_target="tpu_custom_call" | custom-call | flops 7797473280 | bytes 16777216 | tf_op jit(solution)/shard_map/pallas_call | solution.py:354
  216.2 3.6 %copy.10 = bf16[512,2880]{0,1:T(8,128)(2,1)} copy(bf16[512,2880]{0,1:T(8,128)(2,1)} %bitcast.12) | data formatting | bytes 5898240

commit v2 on v1

--- a/solution.py
+++ b/solution.py
@@ -31,7 +31,6 @@
     weight_out_ref,
     x_ref,
     normed,
-    adapted,
     arrived,
     gain_col,
     square_sum,
@@ -42,6 +41,10 @@
     expert_sum,
     expert_own,
     expert_in,
+    raw_rows,
+    low_own,
+    low_in,
+    up_previous,
     meta_own,
     meta_in,
     down_v,
@@ -59,6 +62,10 @@
     e_recv,
     m_send,
     m_recv,
+    l_send,
+    l_recv,
+    u_send,
+    u_recv,
 ):
     section = lax.axis_index("section")
     expert = lax.axis_index("expert")
@@ -134,9 +141,6 @@
             device_id_type=pl.DeviceIdType.MESH,
         )
 
-    meta_copy = remote(meta_own, meta_in, m_send, m_recv, place(following, expert))
-    meta_copy.start()
-
     def tiles(body):
         def step(i, carry):
             body(pl.ds(pl.multiple_of(i * tile, tile), tile))
@@ -144,20 +148,65 @@
 
         lax.fori_loop(0, width // tile, step, 0)
 
-    def add_squares(values):
-        square_sum[...] += jnp.sum((values * values).reshape(tile // 8, 8, rows), axis=0)
+    pieces = [(start, min(start + 768, width)) for start in range(0, width, 768)]
+
+    def lane_tiles(start, stop):
+        return [(at, min(at + 384, stop)) for at in range(start, stop, 384)]
+
+    def stream_copy(hop, c):
+        start, stop = pieces[c]
+        return remote(
+            x_ref.at[start:stop],
+            arrived.at[hop, start:stop],
+            x_send.at[hop, c],
+            x_recv.at[hop, c],
+            place(following, expert),
+        )
 
     loads[0].wait()
-    square_sum[...] = jnp.zeros_like(square_sum)
-
-    def first_squares(at):
-        add_squares(x_ref[at, :].astype(jnp.float32))
-
-    tiles(first_squares)
+    for c in range(len(pieces)):
+        stream_copy(0, c).start()
+    meta_copy = remote(meta_own, meta_in, m_send, m_recv, place(following, expert))
+    meta_copy.start()
+    loads[2].wait()
+    up_copy = remote(up_v, up_previous, u_send, u_recv, place(following, expert))
+    up_copy.start()
 
     def one_hot(meta, hop):
         slots = lax.broadcasted_iota(jnp.int32, (CAP, rows), 0).astype(jnp.float32)
         return jnp.where(slots == meta[hop, 0:1, :], 1.0, 0.0).astype(jnp.bfloat16)
+
+    def select_rows(select, values):
+        return lax.dot_general(
+            select, values, (((1,), (1,)), ((), ())), preferred_element_type=jnp.float32
+        )
+
+    raw_rows[...] = select_rows(one_hot(meta_own, 0), x_ref[...])
+
+    def settle(hop, send_on):
+        spread = one_hot(meta_in, hop)
+        share = meta_in[hop, 1:2, :]
+        square_sum[...] = jnp.zeros_like(square_sum)
+        for c, (first, last) in enumerate(pieces):
+            stream_copy(hop, c).wait_send()
+            for start, stop in lane_tiles(first, last):
+                picked = lax.dot_general(
+                    expert_in[hop, :, start:stop],
+                    spread,
+                    (((0,), (0,)), ((), ())),
+                    preferred_element_type=jnp.float32,
+                )
+                moved = (
+                    arrived[hop, start:stop, :].astype(jnp.float32) + share * picked
+                ).astype(jnp.bfloat16)
+                x_ref[start:stop, :] = moved
+                if send_on:
+                    values = moved.astype(jnp.float32)
+                    square_sum[...] += jnp.sum(
+                        (values * values).reshape((stop - start) // 8, 8, rows), axis=0
+                    )
+            if send_on:
+                stream_copy(hop + 1, c).start()
 
     def expert_partial(block):
         gate = lax.dot_general(
@@ -208,6 +257,31 @@
         return left_at(distance) if side == LEFT else right_at(distance)
 
     def hop_body(hop, carry):
+        raw = raw_rows[...]
+        row_scale = lax.rsqrt(
+            jnp.sum(raw * raw, axis=1, keepdims=True) * (1.0 / width) + 1e-05
+        )
+        own_rows[hop] = (raw * row_scale * gain_ref[...]).astype(jnp.bfloat16)
+        for valid, copy in gather_sends(hop, 0):
+            pl.when(valid)(copy.start)
+
+        @pl.when(hop == 0)
+        def _():
+            square_sum[...] = jnp.zeros_like(square_sum)
+
+            def first_squares(at):
+                values = x_ref[at, :].astype(jnp.float32)
+                square_sum[...] += jnp.sum(
+                    (values * values).reshape(tile // 8, 8, rows), axis=0
+                )
+
+            tiles(first_squares)
+            loads[1].wait()
+
+        @pl.when(hop > 0)
+        def _():
+            settle(hop - 1, True)
+
         scale = lax.rsqrt(
             jnp.sum(square_sum[...], axis=0, keepdims=True) * (1.0 / width) + 1e-05
         )
@@ -217,35 +291,13 @@
             normed[at, :] = (x_ref[at, :].astype(jnp.float32) * scale * gain).astype(jnp.bfloat16)
 
         tiles(normalise)
-        own_rows[hop] = lax.dot_general(
-            one_hot(meta_own, hop),
-            normed[...],
-            (((1,), (1,)), ((), ())),
-            preferred_element_type=jnp.float32,
-        ).astype(jnp.bfloat16)
-        for valid, copy in gather_sends(hop, 0):
-            pl.when(valid)(copy.start)
-
-        @pl.when(hop == 0)
-        def _():
-            loads[1].wait()
-            loads[2].wait()
-
-        low = lax.dot_general(
+        low_own[hop] = lax.dot_general(
             down_v[...], normed[...], (((0,), (0,)), ((), ())), preferred_element_type=jnp.float32
         ).astype(jnp.bfloat16)
-
-        def adapt(at):
-            adapted[at, :] = (
-                x_ref[at, :].astype(jnp.float32)
-                + jnp.dot(up_v[at, :], low, preferred_element_type=jnp.float32)
-            ).astype(jnp.bfloat16)
-
-        tiles(adapt)
-        stream_copy = remote(
-            adapted, arrived.at[hop], x_send.at[hop], x_recv.at[hop], place(following, expert)
-        )
-        stream_copy.start()
+        low_copy = remote(
+            low_own.at[hop], low_in.at[hop], l_send.at[hop], l_recv.at[hop], place(following, expert)
+        )
+        low_copy.start()
 
         def take_and_forward(k):
             for side in (LEFT, RIGHT):
@@ -273,6 +325,34 @@
                 pl.when(on_side(side, k + 1))(partial_send(hop, k, side).start)
             if k + 1 < steps:
                 take_and_forward(k + 1)
+
+        @pl.when(hop == 0)
+        def _():
+            meta_copy.wait()
+            up_copy.wait()
+
+        low_copy.wait()
+        more = hop + 1 < hops
+
+        def adapt(c):
+            first, last = pieces[c]
+            stream_copy(hop, c).wait_recv()
+            for start, stop in lane_tiles(first, last):
+                arrived[hop, start:stop, :] = (
+                    arrived[hop, start:stop, :].astype(jnp.float32)
+                    + jnp.dot(
+                        up_previous[start:stop, :], low_in[hop], preferred_element_type=jnp.float32
+                    )
+                ).astype(jnp.bfloat16)
+
+            @pl.when(more)
+            def _():
+                raw_rows[:, first:last] = select_rows(
+                    one_hot(meta_own, hop + 1), arrived[hop, first:last, :]
+                )
+
+        for c in range(len(pieces) - 1):
+            adapt(c)
 
         for k in range(steps):
             for side in (LEFT, RIGHT):
@@ -291,6 +371,7 @@
             place(following, expert),
         )
         expert_copy.start()
+        adapt(len(pieces) - 1)
 
         for k in range(steps):
             for valid, copy in gather_sends(hop, k):
@@ -298,35 +379,27 @@
             for side in (LEFT, RIGHT):
                 pl.when(on_side(side, k + 1))(partial_send(hop, k, side).wait_send)
 
-        @pl.when(hop == 0)
+        @pl.when(more)
         def _():
-            meta_copy.wait()
-
-        stream_copy.wait()
-        expert_copy.wait()
-        spread = one_hot(meta_in, hop)
-        share = meta_in[hop, 1:2, :]
-        square_sum[...] = jnp.zeros_like(square_sum)
-        lanes = 384
-        for start in range(0, width, lanes):
-            stop = min(start + lanes, width)
-            picked = lax.dot_general(
-                expert_in[hop, :, start:stop],
-                spread,
-                (((0,), (0,)), ((), ())),
-                preferred_element_type=jnp.float32,
+            chosen = one_hot(meta_own, hop + 1)
+            meeting = select_rows(chosen, one_hot(meta_in, hop)).astype(jnp.bfloat16)
+            share = jnp.sum(
+                chosen.astype(jnp.float32) * meta_in[hop, 1:2, :], axis=1, keepdims=True
             )
-            moved = (
-                arrived[hop, start:stop, :].astype(jnp.float32) + share * picked
-            ).astype(jnp.bfloat16)
-            x_ref[start:stop, :] = moved
-            values = moved.astype(jnp.float32)
-            square_sum[...] += jnp.sum(
-                (values * values).reshape((stop - start) // 8, 8, rows), axis=0
+            expert_copy.wait()
+            picked = jnp.dot(meeting, expert_in[hop], preferred_element_type=jnp.float32)
+            raw_rows[...] = (
+                (raw_rows[...] + share * picked).astype(jnp.bfloat16).astype(jnp.float32)
             )
+
+        @pl.when(hop + 1 == hops)
+        def _():
+            expert_copy.wait()
+
         return carry
 
     lax.fori_loop(0, hops, hop_body, 0)
+    settle(hops - 1, False)
 
 
 def body(
@@ -346,6 +419,7 @@
     rank = adapter_down_weight.shape[2]
     hid = expert_down_weight.shape[1]
     steps = n_expert - 1
+    stream_pieces = pl.cdiv(width, 768)
     half = jnp.bfloat16
     full = jnp.float32
     block = (CAP, width)
@@ -367,7 +441,6 @@
         out_specs=pl.BlockSpec(memory_space=pltpu.VMEM),
         scratch_shapes=[
             pltpu.VMEM((width, rows), half),
-            pltpu.VMEM((width, rows), half),
             pltpu.VMEM((hops, width, rows), half),
             pltpu.VMEM((width, 128), full),
             pltpu.VMEM((8, rows), full),
@@ -378,6 +451,10 @@
             pltpu.VMEM(block, full),
             pltpu.VMEM((hops,) + block, half),
             pltpu.VMEM((hops,) + block, half),
+            pltpu.VMEM(block, full),
+            pltpu.VMEM((hops, rank, rows), half),
+            pltpu.VMEM((hops, rank, rows), half),
+            pltpu.VMEM((width, rank), half),
             pltpu.VMEM((hops, 8, rows), full),
             pltpu.VMEM((hops, 8, rows), full),
             pltpu.VMEM((width, rank), half),
@@ -389,8 +466,12 @@
             dma((hops, steps, 2)),
             dma((hops, steps, 2)),
             dma((hops, steps, 2)),
+            dma((hops, stream_pieces)),
+            dma((hops, stream_pieces)),
             dma((hops,)),
             dma((hops,)),
+            dma,
+            dma,
             dma((hops,)),
             dma((hops,)),
             dma,

time: 220 us -> 220 us (level)
  no operation moved by 1% of the time
where the time goes in v2:
time: 220 us; the launch traced here: 219 us
  Pallas kernels  216 us (98%)
  local copies, waits for them, and re-layouts  3.62 us (2%)
    pallas_call x1, Pallas kernels, body(): pl.pallas_call(functools.partial(relay_kernel, n_section, n_expert), out_...  216 us

profile of v2, /device:TPU:24, one launch (start us, length us, event | category | flops | bytes accessed | tf_op | source)
XLA Modules:
  0.0 219.4 jit_solution(17825680764441404730)
XLA Ops:
  0.0 215.7 %shard_map.82 = bf16[2880,512]{1,0:T(8,128)(2,1)} custom-call(bf16[2880,512]{1,0:T(8,128)(2,1)} %bitcast.14, f32[1,2880]{1,0:T(1,128)} %gain_ref.1, s32[4,4,512]{2,1,0:T(4,128)} %bitcast.18, bf16[4,4,512]{2,1,0:T(4,128)(2,1)} %bitcast.19, bf16[2880,128]{1,0:T(8,128)(2,1)} %bitcast.16, bf16[2880,128]{1,0:T(8,128)(2,1)} %bitcast.17, ...), custom_call_target="tpu_custom_call" | custom-call | flops 7797473280 | bytes 16777216 | tf_op jit(solution)/shard_map/pallas_call | solution.py:428
  215.8 3.6 %copy.10 = bf16[512,2880]{0,1:T(8,128)(2,1)} copy(bf16[512,2880]{0,1:T(8,128)(2,1)} %bitcast.12) | data formatting | bytes 5898240

commit v3 on v2

--- a/solution.py
+++ b/solution.py
@@ -8,6 +8,7 @@
 from jax.sharding import PartitionSpec as P
 
 CAP = 48
+ROWS = 16
 LEFT, RIGHT = 0, 1
 
 
@@ -38,6 +39,7 @@
     gathered,
     partials,
     returned,
+    relayed,
     expert_sum,
     expert_own,
     expert_in,
@@ -56,6 +58,7 @@
     ag_recv,
     rs_send,
     rs_recv,
+    relay_recv,
     x_send,
     x_recv,
     e_send,
@@ -243,15 +246,39 @@
             (right_at(k) & left_at(1), gather_send(hop, k, RIGHT)),
         )
 
-    def partial_send(hop, k, side):
+    def piece_of(c):
+        return slice(c * ROWS, (c + 1) * ROWS)
+
+    def partial_send(hop, k, side, c):
         away = -(k + 1) if side == LEFT else k + 1
         return remote(
-            partials.at[k, side],
-            returned.at[hop, k, 1 - side],
-            rs_send.at[hop, k, side],
-            rs_recv.at[hop, k, 1 - side],
+            partials.at[k, side, piece_of(c)],
+            returned.at[hop, k, 1 - side, piece_of(c)],
+            rs_send.at[hop, k, side, c],
+            rs_recv.at[hop, k, 1 - side, c],
             place(section, lax.rem(expert + away + n_expert, n_expert)),
         )
+
+    def relay_send(hop, k, side, c):
+        away = -1 if side == LEFT else 1
+        return remote(
+            partials.at[k, side, piece_of(c)],
+            relayed.at[hop, k - 1, side, piece_of(c)],
+            rs_send.at[hop, k, side, c],
+            relay_recv.at[hop, k - 1, side, c],
+            place(section, lax.rem(expert + away + n_expert, n_expert)),
+        )
+
+    def at_end(side):
+        return expert == (n_expert - 1 if side == LEFT else 0)
+
+    def beside_end(side):
+        return expert == (n_expert - 2 if side == LEFT else 1)
+
+    def sends_here(k, side):
+        if k == 0:
+            return on_side(side, 1)
+        return (expert >= k + 2) if side == LEFT else (expert + k + 2 < n_expert)
 
     def on_side(side, distance):
         return left_at(distance) if side == LEFT else right_at(distance)
@@ -322,9 +349,37 @@
                 partials[k] = expert_partial(block).reshape(2, CAP, width)
 
             for side in (LEFT, RIGHT):
-                pl.when(on_side(side, k + 1))(partial_send(hop, k, side).start)
+                valid = on_side(side, k + 1)
+                straight = valid & jnp.logical_not(beside_end(side))
+                if k > 0:
+                    straight = straight & jnp.logical_not(at_end(side))
+
+                    @pl.when(valid & at_end(side))
+                    def _(k=k, side=side):
+                        for c in range(CAP // ROWS):
+                            relay_send(hop, k, side, c).start()
+
+                @pl.when(straight)
+                def _(k=k, side=side):
+                    for c in range(CAP // ROWS):
+                        partial_send(hop, k, side, c).start()
+
             if k + 1 < steps:
                 take_and_forward(k + 1)
+
+        for k in range(steps - 1):
+            for side in (LEFT, RIGHT):
+
+                @pl.when(on_side(side, k + 1) & beside_end(side))
+                def _(k=k, side=side):
+                    for c in range(CAP // ROWS):
+                        relay_send(hop, k + 1, side, c).wait_recv()
+                        at = piece_of(c)
+                        partials[k, side, at] = (
+                            partials[k, side, at].astype(jnp.float32)
+                            + relayed[hop, k, side, at].astype(jnp.float32)
+                        ).astype(jnp.bfloat16)
+                        partial_send(hop, k, side, c).start()
 
         @pl.when(hop == 0)
         def _():
@@ -357,9 +412,10 @@
         for k in range(steps):
             for side in (LEFT, RIGHT):
 
-                @pl.when(on_side(side, k + 1))
+                @pl.when(sends_here(k, side))
                 def _(k=k, side=side):
-                    partial_send(hop, k, 1 - side).wait_recv()
+                    for c in range(CAP // ROWS):
+                        partial_send(hop, k, 1 - side, c).wait_recv()
                     expert_sum[...] += returned[hop, k, side].astype(jnp.float32)
 
         expert_own[hop] = expert_sum[...].astype(jnp.bfloat16)
@@ -377,7 +433,8 @@
             for valid, copy in gather_sends(hop, k):
                 pl.when(valid)(copy.wait_send)
             for side in (LEFT, RIGHT):
-                pl.when(on_side(side, k + 1))(partial_send(hop, k, side).wait_send)
+                for c in range(CAP // ROWS):
+                    pl.when(on_side(side, k + 1))(partial_send(hop, k, side, c).wait_send)
 
         @pl.when(more)
         def _():
@@ -448,6 +505,7 @@
             pltpu.VMEM((hops, steps, 2) + block, half),
             pltpu.VMEM((steps, 2) + block, half),
             pltpu.VMEM((hops, steps, 2) + block, half),
+            pltpu.VMEM((hops, steps - 1, 2) + block, half),
             pltpu.VMEM(block, full),
             pltpu.VMEM((hops,) + block, half),
             pltpu.VMEM((hops,) + block, half),
@@ -464,8 +522,9 @@
             dma((5,)),
             dma((hops, steps, 2)),
             dma((hops, steps, 2)),
-            dma((hops, steps, 2)),
-            dma((hops, steps, 2)),
+            dma((hops, steps, 2, CAP // ROWS)),
+            dma((hops, steps, 2, CAP // ROWS)),
+            dma((hops, steps - 1, 2, CAP // ROWS)),
             dma((hops, stream_pieces)),
             dma((hops, stream_pieces)),
             dma((hops,)),

time: 220 us -> 186 us (0.85); the launches traced: 219 us -> 182 us
  Pallas kernels: 216 us -> 179 us
    pallas_call x1, Pallas kernels: 216 us -> 179 us  [body(): pl.pallas_call(functools.partial(relay_kernel, n_section, n_expert), out_...]
where the time goes in v3:
time: 186 us; the launch traced here: 182 us
  Pallas kernels  179 us (96%)
  local copies, waits for them, and re-layouts  3.62 us (2%)
    pallas_call x1, Pallas kernels, body(): pl.pallas_call(functools.partial(relay_kernel, n_section, n_expert), out_...  179 us

profile of v3, /device:TPU:24, one launch (start us, length us, event | category | flops | bytes accessed | tf_op | source)
XLA Modules:
  0.0 182.4 jit_solution(9019204056575662286)
XLA Ops:
  0.0 178.8 %shard_map.82 = bf16[2880,512]{1,0:T(8,128)(2,1)} custom-call(bf16[2880,512]{1,0:T(8,128)(2,1)} %bitcast.14, f32[1,2880]{1,0:T(1,128)} %gain_ref.1, s32[4,4,512]{2,1,0:T(4,128)} %bitcast.18, bf16[4,4,512]{2,1,0:T(4,128)(2,1)} %bitcast.19, bf16[2880,128]{1,0:T(8,128)(2,1)} %bitcast.16, bf16[2880,128]{1,0:T(8,128)(2,1)} %bitcast.17, ...), custom_call_target="tpu_custom_call" | custom-call | flops 7797473280 | bytes 16777216 | tf_op jit(solution)/shard_map/pallas_call | solution.py:485
  178.8 3.6 %copy.10 = bf16[512,2880]{0,1:T(8,128)(2,1)} copy(bf16[512,2880]{0,1:T(8,128)(2,1)} %bitcast.12) | data formatting | bytes 5898240

commit v4 on v3

--- a/solution.py
+++ b/solution.py
@@ -30,6 +30,9 @@
     up_ref,
     weight_in_ref,
     weight_out_ref,
+    out_ref,
+    last_sum_ref,
+    last_meta_ref,
     x_ref,
     normed,
     arrived,
@@ -69,6 +72,7 @@
     l_recv,
     u_send,
     u_recv,
+    out_sem,
 ):
     section = lax.axis_index("section")
     expert = lax.axis_index("expert")
@@ -127,11 +131,6 @@
         meta_own[hop, 0:1, :] = jnp.where(flag > 0.0, position, float(CAP))
         meta_own[hop, 1:2, :] = chosen / total
 
-    for start in range(0, width, 128):
-        stop = min(start + 128, width)
-        piece = jnp.broadcast_to(gain_ref[0:1, start:stop], (128, stop - start))
-        gain_col[start:stop, :] = piece.T
-
     pl.semaphore_wait(barrier, 5)
 
     def remote(source, target, send, recv, device):
@@ -175,6 +174,16 @@
     up_copy = remote(up_v, up_previous, u_send, u_recv, place(following, expert))
     up_copy.start()
 
+    def expert_copy(hop, c):
+        at = slice(c * ROWS, (c + 1) * ROWS)
+        return remote(
+            expert_own.at[hop, at],
+            expert_in.at[hop, at],
+            e_send.at[hop, c],
+            e_recv.at[hop, c],
+            place(following, expert),
+        )
+
     def one_hot(meta, hop):
         slots = lax.broadcasted_iota(jnp.int32, (CAP, rows), 0).astype(jnp.float32)
         return jnp.where(slots == meta[hop, 0:1, :], 1.0, 0.0).astype(jnp.bfloat16)
@@ -186,7 +195,7 @@
 
     raw_rows[...] = select_rows(one_hot(meta_own, 0), x_ref[...])
 
-    def settle(hop, send_on):
+    def settle(hop):
         spread = one_hot(meta_in, hop)
         share = meta_in[hop, 1:2, :]
         square_sum[...] = jnp.zeros_like(square_sum)
@@ -203,13 +212,17 @@
                     arrived[hop, start:stop, :].astype(jnp.float32) + share * picked
                 ).astype(jnp.bfloat16)
                 x_ref[start:stop, :] = moved
-                if send_on:
-                    values = moved.astype(jnp.float32)
-                    square_sum[...] += jnp.sum(
-                        (values * values).reshape((stop - start) // 8, 8, rows), axis=0
-                    )
-            if send_on:
-                stream_copy(hop + 1, c).start()
+                values = moved.astype(jnp.float32)
+                square_sum[...] += jnp.sum(
+                    (values * values).reshape((stop - start) // 8, 8, rows), axis=0
+                )
+            stream_copy(hop + 1, c).start()
+
+    def write_out(c):
+        start, stop = pieces[c]
+        return pltpu.make_async_copy(
+            arrived.at[hops - 1, start:stop], out_ref.at[start:stop], out_sem.at[c]
+        )
 
     def expert_partial(block):
         gate = lax.dot_general(
@@ -303,11 +316,15 @@
                 )
 
             tiles(first_squares)
+            for start in range(0, width, 128):
+                stop = min(start + 128, width)
+                piece = jnp.broadcast_to(gain_ref[0:1, start:stop], (128, stop - start))
+                gain_col[start:stop, :] = piece.T
             loads[1].wait()
 
         @pl.when(hop > 0)
         def _():
-            settle(hop - 1, True)
+            settle(hop - 1)
 
         scale = lax.rsqrt(
             jnp.sum(square_sum[...], axis=0, keepdims=True) * (1.0 / width) + 1e-05
@@ -406,27 +423,26 @@
                     one_hot(meta_own, hop + 1), arrived[hop, first:last, :]
                 )
 
+            @pl.when(hop + 1 == hops)
+            def _():
+                write_out(c).start()
+
         for c in range(len(pieces) - 1):
             adapt(c)
 
-        for k in range(steps):
-            for side in (LEFT, RIGHT):
-
-                @pl.when(sends_here(k, side))
-                def _(k=k, side=side):
-                    for c in range(CAP // ROWS):
+        for c in range(CAP // ROWS):
+            at = piece_of(c)
+            for k in range(steps):
+                for side in (LEFT, RIGHT):
+
+                    @pl.when(sends_here(k, side))
+                    def _(k=k, side=side, c=c, at=at):
                         partial_send(hop, k, 1 - side, c).wait_recv()
-                    expert_sum[...] += returned[hop, k, side].astype(jnp.float32)
-
-        expert_own[hop] = expert_sum[...].astype(jnp.bfloat16)
-        expert_copy = remote(
-            expert_own.at[hop],
-            expert_in.at[hop],
-            e_send.at[hop],
-            e_recv.at[hop],
-            place(following, expert),
-        )
-        expert_copy.start()
+                        expert_sum[at] += returned[hop, k, side, at].astype(jnp.float32)
+
+            expert_own[hop, at] = expert_sum[at].astype(jnp.bfloat16)
+            expert_copy(hop, c).start()
+
         adapt(len(pieces) - 1)
 
         for k in range(steps):
@@ -443,7 +459,8 @@
             share = jnp.sum(
                 chosen.astype(jnp.float32) * meta_in[hop, 1:2, :], axis=1, keepdims=True
             )
-            expert_copy.wait()
+            for c in range(CAP // ROWS):
+                expert_copy(hop, c).wait()
             picked = jnp.dot(meeting, expert_in[hop], preferred_element_type=jnp.float32)
             raw_rows[...] = (
                 (raw_rows[...] + share * picked).astype(jnp.bfloat16).astype(jnp.float32)
@@ -451,12 +468,29 @@
 
         @pl.when(hop + 1 == hops)
         def _():
-            expert_copy.wait()
+            for c in range(CAP // ROWS):
+                expert_copy(hop, c).wait()
 
         return carry
 
     lax.fori_loop(0, hops, hop_body, 0)
-    settle(hops - 1, False)
+    last_sum_ref[...] = expert_in[hops - 1]
+    last_meta_ref[...] = meta_in[hops - 1]
+    for c in range(len(pieces)):
+        stream_copy(hops - 1, c).wait_send()
+        write_out(c).wait()
+
+
+def last_kernel(adapted_ref, expert_ref, meta_ref, out_ref):
+    rows = out_ref.shape[1]
+    slots = lax.broadcasted_iota(jnp.int32, (CAP, rows), 0).astype(jnp.float32)
+    spread = jnp.where(slots == meta_ref[0:1, :], 1.0, 0.0).astype(jnp.bfloat16)
+    picked = lax.dot_general(
+        expert_ref[...], spread, (((0,), (0,)), ((), ())), preferred_element_type=jnp.float32
+    )
+    out_ref[...] = (
+        adapted_ref[...].astype(jnp.float32) + meta_ref[1:2, :] * picked
+    ).astype(out_ref.dtype)
 
 
 def body(
@@ -482,9 +516,13 @@
     block = (CAP, width)
     dma = pltpu.SemaphoreType.DMA
     flops = hops * (4 * rows * width * rank + 6 * n_expert * CAP * width * hid)
-    out = pl.pallas_call(
+    adapted, last_sum, last_meta = pl.pallas_call(
         functools.partial(relay_kernel, n_section, n_expert),
-        out_shape=jax.ShapeDtypeStruct((width, rows), half),
+        out_shape=(
+            jax.ShapeDtypeStruct((width, rows), half),
+            jax.ShapeDtypeStruct(block, half),
+            jax.ShapeDtypeStruct((8, rows), full),
+        ),
         in_specs=[
             pl.BlockSpec(memory_space=pl.ANY),
             pl.BlockSpec(memory_space=pltpu.VMEM),
@@ -495,8 +533,13 @@
             pl.BlockSpec(memory_space=pl.ANY),
             pl.BlockSpec(memory_space=pl.ANY),
         ],
-        out_specs=pl.BlockSpec(memory_space=pltpu.VMEM),
+        out_specs=(
+            pl.BlockSpec(memory_space=pl.ANY),
+            pl.BlockSpec(memory_space=pltpu.VMEM),
+            pl.BlockSpec(memory_space=pltpu.VMEM),
+        ),
         scratch_shapes=[
+            pltpu.VMEM((width, rows), half),
             pltpu.VMEM((width, rows), half),
             pltpu.VMEM((hops, width, rows), half),
             pltpu.VMEM((width, 128), full),
@@ -527,14 +570,15 @@
             dma((hops, steps - 1, 2, CAP // ROWS)),
             dma((hops, stream_pieces)),
             dma((hops, stream_pieces)),
-            dma((hops,)),
-            dma((hops,)),
+            dma((hops, CAP // ROWS)),
+            dma((hops, CAP // ROWS)),
             dma,
             dma,
             dma((hops,)),
             dma((hops,)),
             dma,
             dma,
+            dma((stream_pieces,)),
         ],
         compiler_params=pltpu.CompilerParams(
             collective_id=0, has_side_effects=True, vmem_limit_bytes=60 * 2**20
@@ -552,6 +596,21 @@
         jnp.transpose(expert_gate_up_weight[0], (1, 2, 0)),
         expert_down_weight[0],
     )
+    lanes = 384
+    out = pl.pallas_call(
+        last_kernel,
+        out_shape=jax.ShapeDtypeStruct((width, rows), half),
+        grid=(pl.cdiv(width, lanes),),
+        in_specs=[
+            pl.BlockSpec((lanes, rows), lambda i: (i, 0)),
+            pl.BlockSpec((CAP, lanes), lambda i: (0, i)),
+            pl.BlockSpec((8, rows), lambda i: (0, 0)),
+        ],
+        out_specs=pl.BlockSpec((lanes, rows), lambda i: (i, 0)),
+        cost_estimate=pl.CostEstimate(
+            flops=2 * CAP * width * rows, bytes_accessed=4 * width * rows, transcendentals=0
+        ),
+    )(adapted, last_sum, last_meta)
     return out.T
 
 

time: 186 us -> 186 us (level)
  Pallas kernels: 179 us -> 183 us
  local copies, waits for them, and re-layouts: 3.62 us -> 0 us
    pallas_call x0 -> x1, Pallas kernels: none -> 6.92 us  [body(): pl.pallas_call(last_kernel, out_shape=jax.ShapeDtypeStruct((width, rows),...]
    unnamed x1 -> x0, local copies, waits for them, and re-layouts: 3.62 us -> none
    pallas_call x1, Pallas kernels: 179 us -> 176 us  [body(): pl.pallas_call(functools.partial(relay_kernel, n_section, n_expert), out_...]
where the time goes in v4:
time: 186 us; the launch traced here: 183 us
  Pallas kernels  183 us (98%)
    pallas_call x1, Pallas kernels, body(): pl.pallas_call(functools.partial(relay_kernel, n_section, n_expert), out_...  176 us
    pallas_call x1, Pallas kernels, body(): pl.pallas_call(last_kernel, out_shape=jax.ShapeDtypeStruct((width, rows),...  6.92 us

profile of v4, /device:TPU:24, one launch (start us, length us, event | category | flops | bytes accessed | tf_op | source)
XLA Modules:
  0.0 183.0 jit_solution(13639508734945737173)
XLA Ops:
  0.0 176.1 %shard_map.82 = (bf16[2880,512]{1,0:T(8,128)(2,1)}, bf16[48,2880]{1,0:T(8,128)(2,1)}, f32[8,512]{1,0:T(8,128)}) custom-call(bf16[2880,512]{1,0:T(8,128)(2,1)} %bitcast.13, f32[1,2880]{1,0:T(1,128)} %gain_ref.1, s32[4,4,512]{2,1,0:T(4,128)} %bitcast.17, bf16[4,4,512]{2,1,0:T(4,128)(2,1)} %bitcast.18, bf16[2880,128]{1,0:T(8,128)(2,1)} %bitcast.15, ...), custom_call_target="tpu_custom_call" | custom-call | flops 7797473280 | bytes 16777216 | tf_op jit(solution)/shard_map/pallas_call | solution.py:519
  176.1 6.9 %shard_map.83 = bf16[2880,512]{1,0:T(8,128)(2,1)} custom-call(bf16[2880,512]{1,0:T(8,128)(2,1)} %get-tuple-element.8.adapted_ref, bf16[48,2880]{1,0:T(8,128)(2,1)} %get-tuple-element.9.expert_ref, f32[8,512]{1,0:T(8,128)} %get-tuple-element.10.meta_ref), custom_call_target="tpu_custom_call" | custom-call | flops 141557760 | bytes 5898240 | tf_op jit(solution)/shard_map/pallas_call | solution.py:600

commit v5 on v4

--- a/solution.py
+++ b/solution.py
@@ -111,6 +111,49 @@
     ):
         pl.semaphore_signal(barrier, inc=1, device_id=target, device_id_type=pl.DeviceIdType.MESH)
 
+    pl.semaphore_wait(barrier, 5)
+
+    def remote(source, target, send, recv, device):
+        return pltpu.make_async_remote_copy(
+            src_ref=source,
+            dst_ref=target,
+            send_sem=send,
+            recv_sem=recv,
+            device_id=device,
+            device_id_type=pl.DeviceIdType.MESH,
+        )
+
+    def tiles(body):
+        def step(i, carry):
+            body(pl.ds(pl.multiple_of(i * tile, tile), tile))
+            return carry
+
+        lax.fori_loop(0, width // tile, step, 0)
+
+    pieces = [(start, min(start + 768, width)) for start in range(0, width, 768)]
+
+    def lane_tiles(start, stop):
+        return [(at, min(at + 384, stop)) for at in range(start, stop, 384)]
+
+    def stream_copy(hop, c):
+        start, stop = pieces[c]
+        return remote(
+            x_ref.at[start:stop],
+            arrived.at[hop, start:stop],
+            x_send.at[hop, c],
+            x_recv.at[hop, c],
+            place(following, expert),
+        )
+
+    loads[0].wait()
+    stream_copy(0, 0).start()
+    loads[2].wait()
+    first_rows = pieces[0][1]
+    up_copy = remote(
+        up_v.at[0:first_rows], up_previous, u_send, u_recv, place(following, expert)
+    )
+    up_copy.start()
+
     before = (
         lax.broadcasted_iota(jnp.int32, (rows, rows), 0)
         < lax.broadcasted_iota(jnp.int32, (rows, rows), 1)
@@ -131,48 +174,8 @@
         meta_own[hop, 0:1, :] = jnp.where(flag > 0.0, position, float(CAP))
         meta_own[hop, 1:2, :] = chosen / total
 
-    pl.semaphore_wait(barrier, 5)
-
-    def remote(source, target, send, recv, device):
-        return pltpu.make_async_remote_copy(
-            src_ref=source,
-            dst_ref=target,
-            send_sem=send,
-            recv_sem=recv,
-            device_id=device,
-            device_id_type=pl.DeviceIdType.MESH,
-        )
-
-    def tiles(body):
-        def step(i, carry):
-            body(pl.ds(pl.multiple_of(i * tile, tile), tile))
-            return carry
-
-        lax.fori_loop(0, width // tile, step, 0)
-
-    pieces = [(start, min(start + 768, width)) for start in range(0, width, 768)]
-
-    def lane_tiles(start, stop):
-        return [(at, min(at + 384, stop)) for at in range(start, stop, 384)]
-
-    def stream_copy(hop, c):
-        start, stop = pieces[c]
-        return remote(
-            x_ref.at[start:stop],
-            arrived.at[hop, start:stop],
-            x_send.at[hop, c],
-            x_recv.at[hop, c],
-            place(following, expert),
-        )
-
-    loads[0].wait()
-    for c in range(len(pieces)):
-        stream_copy(0, c).start()
     meta_copy = remote(meta_own, meta_in, m_send, m_recv, place(following, expert))
     meta_copy.start()
-    loads[2].wait()
-    up_copy = remote(up_v, up_previous, u_send, u_recv, place(following, expert))
-    up_copy.start()
 
     def expert_copy(hop, c):
         at = slice(c * ROWS, (c + 1) * ROWS)
@@ -183,6 +186,12 @@
             e_recv.at[hop, c],
             place(following, expert),
         )
+
+    def add_adapter(rows_ref, up_rows, low):
+        rows_ref[...] = (
+            rows_ref[...].astype(jnp.float32)
+            + jnp.dot(up_rows, low, preferred_element_type=jnp.float32)
+        ).astype(jnp.bfloat16)
 
     def one_hot(meta, hop):
         slots = lax.broadcasted_iota(jnp.int32, (CAP, rows), 0).astype(jnp.float32)
@@ -216,7 +225,8 @@
                 square_sum[...] += jnp.sum(
                     (values * values).reshape((stop - start) // 8, 8, rows), axis=0
                 )
-            stream_copy(hop + 1, c).start()
+            if c == 0:
+                stream_copy(hop + 1, c).start()
 
     def write_out(c):
         start, stop = pieces[c]
@@ -350,7 +360,12 @@
                 for valid, copy in gather_sends(hop, k + 1):
                     pl.when(valid)(copy.start)
 
-        take_and_forward(0)
+        for c in range(1, len(pieces)):
+            for start, stop in lane_tiles(*pieces[c]):
+                add_adapter(x_ref.at[start:stop], up_v[start:stop, :], low_own[hop])
+            stream_copy(hop, c).start()
+            if c == 1:
+                take_and_forward(0)
 
         @pl.when(hop == 0)
         def _():
@@ -409,13 +424,11 @@
         def adapt(c):
             first, last = pieces[c]
             stream_copy(hop, c).wait_recv()
-            for start, stop in lane_tiles(first, last):
-                arrived[hop, start:stop, :] = (
-                    arrived[hop, start:stop, :].astype(jnp.float32)
-                    + jnp.dot(
-                        up_previous[start:stop, :], low_in[hop], preferred_element_type=jnp.float32
+            if c == 0:
+                for start, stop in lane_tiles(first, last):
+                    add_adapter(
+                        arrived.at[hop, start:stop], up_previous[start:stop, :], low_in[hop]
                     )
-                ).astype(jnp.bfloat16)
 
             @pl.when(more)
             def _():
@@ -555,7 +568,7 @@
             pltpu.VMEM(block, full),
             pltpu.VMEM((hops, rank, rows), half),
             pltpu.VMEM((hops, rank, rows), half),
-            pltpu.VMEM((width, rank), half),
+            pltpu.VMEM((min(width, 768), rank), half),
             pltpu.VMEM((hops, 8, rows), full),
             pltpu.VMEM((hops, 8, rows), full),
             pltpu.VMEM((width, rank), half),
@@ -596,7 +609,7 @@
         jnp.transpose(expert_gate_up_weight[0], (1, 2, 0)),
         expert_down_weight[0],
     )
-    lanes = 384
+    lanes = 768
     out = pl.pallas_call(
         last_kernel,
         out_shape=jax.ShapeDtypeStruct((width, rows), half),

time: 186 us -> 188 us (1.011)
  Pallas kernels: 183 us -> 185 us
    pallas_call x1, Pallas kernels: 176 us -> 180 us  [body(): pl.pallas_call(functools.partial(relay_kernel, n_section, n_expert), out_...]
    pallas_call x1, Pallas kernels: 6.92 us -> 4.87 us  [body(): pl.pallas_call(last_kernel, out_shape=jax.ShapeDtypeStruct((width, rows),...]
where the time goes in v5:
time: 188 us; the launch traced here: 185 us
  Pallas kernels  185 us (98%)
    pallas_call x1, Pallas kernels, body(): pl.pallas_call(functools.partial(relay_kernel, n_section, n_expert), out_...  180 us
    pallas_call x1, Pallas kernels, body(): pl.pallas_call(last_kernel, out_shape=jax.ShapeDtypeStruct((width, rows),...  4.87 us

profile of v5, /device:TPU:24, one launch (start us, length us, event | category | flops | bytes accessed | tf_op | source)
XLA Modules:
  0.0 184.9 jit_solution(7129599742735037207)
XLA Ops:
  0.0 180.0 %shard_map.82 = (bf16[2880,512]{1,0:T(8,128)(2,1)}, bf16[48,2880]{1,0:T(8,128)(2,1)}, f32[8,512]{1,0:T(8,128)}) custom-call(bf16[2880,512]{1,0:T(8,128)(2,1)} %bitcast.13, f32[1,2880]{1,0:T(1,128)} %gain_ref.1, s32[4,4,512]{2,1,0:T(4,128)} %bitcast.17, bf16[4,4,512]{2,1,0:T(4,128)(2,1)} %bitcast.18, bf16[2880,128]{1,0:T(8,128)(2,1)} %bitcast.15, ...), custom_call_target="tpu_custom_call" | custom-call | flops 7797473280 | bytes 16777216 | tf_op jit(solution)/shard_map/pallas_call | solution.py:532
  180.0 4.9 %shard_map.83 = bf16[2880,512]{1,0:T(8,128)(2,1)} custom-call(bf16[2880,512]{1,0:T(8,128)(2,1)} %get-tuple-element.8.adapted_ref, bf16[48,2880]{1,0:T(8,128)(2,1)} %get-tuple-element.9.expert_ref, f32[8,512]{1,0:T(8,128)} %get-tuple-element.10.meta_ref), custom_call_target="tpu_custom_call" | custom-call | flops 141557760 | bytes 5898240 | tf_op jit(solution)/shard_map/pallas_call | solution.py:613

commit v6 on v5

--- a/solution.py
+++ b/solution.py
@@ -146,13 +146,8 @@
         )
 
     loads[0].wait()
-    stream_copy(0, 0).start()
-    loads[2].wait()
-    first_rows = pieces[0][1]
-    up_copy = remote(
-        up_v.at[0:first_rows], up_previous, u_send, u_recv, place(following, expert)
-    )
-    up_copy.start()
+    for c in range(len(pieces)):
+        stream_copy(0, c).start()
 
     before = (
         lax.broadcasted_iota(jnp.int32, (rows, rows), 0)
@@ -176,6 +171,9 @@
 
     meta_copy = remote(meta_own, meta_in, m_send, m_recv, place(following, expert))
     meta_copy.start()
+    loads[2].wait()
+    up_copy = remote(up_v, up_previous, u_send, u_recv, place(following, expert))
+    up_copy.start()
 
     def expert_copy(hop, c):
         at = slice(c * ROWS, (c + 1) * ROWS)
@@ -186,12 +184,6 @@
             e_recv.at[hop, c],
             place(following, expert),
         )
-
-    def add_adapter(rows_ref, up_rows, low):
-        rows_ref[...] = (
-            rows_ref[...].astype(jnp.float32)
-            + jnp.dot(up_rows, low, preferred_element_type=jnp.float32)
-        ).astype(jnp.bfloat16)
 
     def one_hot(meta, hop):
         slots = lax.broadcasted_iota(jnp.int32, (CAP, rows), 0).astype(jnp.float32)
@@ -225,8 +217,7 @@
                 square_sum[...] += jnp.sum(
                     (values * values).reshape((stop - start) // 8, 8, rows), axis=0
                 )
-            if c == 0:
-                stream_copy(hop + 1, c).start()
+            stream_copy(hop + 1, c).start()
 
     def write_out(c):
         start, stop = pieces[c]
@@ -345,13 +336,9 @@
             normed[at, :] = (x_ref[at, :].astype(jnp.float32) * scale * gain).astype(jnp.bfloat16)
 
         tiles(normalise)
-        low_own[hop] = lax.dot_general(
-            down_v[...], normed[...], (((0,), (0,)), ((), ())), preferred_element_type=jnp.float32
-        ).astype(jnp.bfloat16)
         low_copy = remote(
             low_own.at[hop], low_in.at[hop], l_send.at[hop], l_recv.at[hop], place(following, expert)
         )
-        low_copy.start()
 
         def take_and_forward(k):
             for side in (LEFT, RIGHT):
@@ -360,19 +347,13 @@
                 for valid, copy in gather_sends(hop, k + 1):
                     pl.when(valid)(copy.start)
 
-        for c in range(1, len(pieces)):
-            for start, stop in lane_tiles(*pieces[c]):
-                add_adapter(x_ref.at[start:stop], up_v[start:stop, :], low_own[hop])
-            stream_copy(hop, c).start()
-            if c == 1:
-                take_and_forward(0)
+        take_and_forward(0)
 
         @pl.when(hop == 0)
         def _():
             loads[3].wait()
             loads[4].wait()
 
-        expert_sum[...] = expert_partial(own_rows[hop]).astype(jnp.float32)
         for k in range(steps):
 
             @pl.when(left_at(k + 1) | right_at(k + 1))
@@ -396,8 +377,16 @@
                     for c in range(CAP // ROWS):
                         partial_send(hop, k, side, c).start()
 
+            if k == 0:
+                low_own[hop] = lax.dot_general(
+                    down_v[...], normed[...], (((0,), (0,)), ((), ())), preferred_element_type=jnp.float32
+                ).astype(jnp.bfloat16)
+                low_copy.start()
+
             if k + 1 < steps:
                 take_and_forward(k + 1)
+
+        expert_sum[...] = expert_partial(own_rows[hop]).astype(jnp.float32)
 
         for k in range(steps - 1):
             for side in (LEFT, RIGHT):
@@ -424,11 +413,13 @@
         def adapt(c):
             first, last = pieces[c]
             stream_copy(hop, c).wait_recv()
-            if c == 0:
-                for start, stop in lane_tiles(first, last):
-                    add_adapter(
-                        arrived.at[hop, start:stop], up_previous[start:stop, :], low_in[hop]
+            for start, stop in lane_tiles(first, last):
+                arrived[hop, start:stop, :] = (
+                    arrived[hop, start:stop, :].astype(jnp.float32)
+                    + jnp.dot(
+                        up_previous[start:stop, :], low_in[hop], preferred_element_type=jnp.float32
                     )
+                ).astype(jnp.bfloat16)
 
             @pl.when(more)
             def _():
@@ -568,7 +559,7 @@
             pltpu.VMEM(block, full),
             pltpu.VMEM((hops, rank, rows), half),
             pltpu.VMEM((hops, rank, rows), half),
-            pltpu.VMEM((min(width, 768), rank), half),
+            pltpu.VMEM((width, rank), half),
             pltpu.VMEM((hops, 8, rows), full),
             pltpu.VMEM((hops, 8, rows), full),
             pltpu.VMEM((width, rank), half),

time: 188 us -> 184 us (0.979)
  Pallas kernels: 185 us -> 181 us
    pallas_call x1, Pallas kernels: 180 us -> 176 us  [body(): pl.pallas_call(functools.partial(relay_kernel, n_section, n_expert), out_...]
where the time goes in v6:
time: 184 us; the launch traced here: 181 us
  Pallas kernels  181 us (98%)
    pallas_call x1, Pallas kernels, body(): pl.pallas_call(functools.partial(relay_kernel, n_section, n_expert), out_...  176 us
    pallas_call x1, Pallas kernels, body(): pl.pallas_call(last_kernel, out_shape=jax.ShapeDtypeStruct((width, rows),...  4.87 us

profile of v6, /device:TPU:24, one launch (start us, length us, event | category | flops | bytes accessed | tf_op | source)
XLA Modules:
  0.0 181.0 jit_solution(6842745296441779762)
XLA Ops:
  0.0 176.1 %shard_map.82 = (bf16[2880,512]{1,0:T(8,128)(2,1)}, bf16[48,2880]{1,0:T(8,128)(2,1)}, f32[8,512]{1,0:T(8,128)}) custom-call(bf16[2880,512]{1,0:T(8,128)(2,1)} %bitcast.13, f32[1,2880]{1,0:T(1,128)} %gain_ref.1, s32[4,4,512]{2,1,0:T(4,128)} %bitcast.17, bf16[4,4,512]{2,1,0:T(4,128)(2,1)} %bitcast.18, bf16[2880,128]{1,0:T(8,128)(2,1)} %bitcast.15, ...), custom_call_target="tpu_custom_call" | custom-call | flops 7797473280 | bytes 16777216 | tf_op jit(solution)/shard_map/pallas_call | solution.py:523
  176.1 4.9 %shard_map.83 = bf16[2880,512]{1,0:T(8,128)(2,1)} custom-call(bf16[2880,512]{1,0:T(8,128)(2,1)} %get-tuple-element.8.adapted_ref, bf16[48,2880]{1,0:T(8,128)(2,1)} %get-tuple-element.9.expert_ref, f32[8,512]{1,0:T(8,128)} %get-tuple-element.10.meta_ref), custom_call_target="tpu_custom_call" | custom-call | flops 141557760 | bytes 5898240 | tf_op jit(solution)/shard_map/pallas_call | solution.py:604

commit v7 on v6

--- a/solution.py
+++ b/solution.py
@@ -9,6 +9,7 @@
 
 CAP = 48
 ROWS = 16
+RAW_PIECES = 2
 LEFT, RIGHT = 0, 1
 
 
@@ -146,7 +147,7 @@
         )
 
     loads[0].wait()
-    for c in range(len(pieces)):
+    for c in range(RAW_PIECES):
         stream_copy(0, c).start()
 
     before = (
@@ -172,7 +173,9 @@
     meta_copy = remote(meta_own, meta_in, m_send, m_recv, place(following, expert))
     meta_copy.start()
     loads[2].wait()
-    up_copy = remote(up_v, up_previous, u_send, u_recv, place(following, expert))
+    first_rows = pieces[RAW_PIECES - 1][1]
+    up_copy = remote(
+        up_v.at[0:first_rows], up_previous, u_send, u_recv, place(following, expert))
     up_copy.start()
 
     def expert_copy(hop, c):
@@ -184,6 +187,12 @@
             e_recv.at[hop, c],
             place(following, expert),
         )
+
+    def add_adapter(rows_ref, up_rows, low):
+        rows_ref[...] = (
+            rows_ref[...].astype(jnp.float32)
+            + jnp.dot(up_rows, low, preferred_element_type=jnp.float32)
+        ).astype(jnp.bfloat16)
 
     def one_hot(meta, hop):
         slots = lax.broadcasted_iota(jnp.int32, (CAP, rows), 0).astype(jnp.float32)
@@ -217,7 +226,8 @@
                 square_sum[...] += jnp.sum(
                     (values * values).reshape((stop - start) // 8, 8, rows), axis=0
                 )
-            stream_copy(hop + 1, c).start()
+            if c < RAW_PIECES:
+                stream_copy(hop + 1, c).start()
 
     def write_out(c):
         start, stop = pieces[c]
@@ -385,6 +395,11 @@
 
             if k + 1 < steps:
                 take_and_forward(k + 1)
+            if k == 0:
+                for c in range(RAW_PIECES, len(pieces)):
+                    for start, stop in lane_tiles(*pieces[c]):
+                        add_adapter(x_ref.at[start:stop], up_v[start:stop, :], low_own[hop])
+                    stream_copy(hop, c).start()
 
         expert_sum[...] = expert_partial(own_rows[hop]).astype(jnp.float32)
 
@@ -413,13 +428,11 @@
         def adapt(c):
             first, last = pieces[c]
             stream_copy(hop, c).wait_recv()
-            for start, stop in lane_tiles(first, last):
-                arrived[hop, start:stop, :] = (
-                    arrived[hop, start:stop, :].astype(jnp.float32)
-                    + jnp.dot(
-                        up_previous[start:stop, :], low_in[hop], preferred_element_type=jnp.float32
+            if c < RAW_PIECES:
+                for start, stop in lane_tiles(first, last):
+                    add_adapter(
+                        arrived.at[hop, start:stop], up_previous[start:stop, :], low_in[hop]
                     )
-                ).astype(jnp.bfloat16)
 
             @pl.when(more)
             def _():
@@ -559,7 +572,7 @@
             pltpu.VMEM(block, full),
             pltpu.VMEM((hops, rank, rows), half),
             pltpu.VMEM((hops, rank, rows), half),
-            pltpu.VMEM((width, rank), half),
+            pltpu.VMEM((min(width, 768 * RAW_PIECES), rank), half),
             pltpu.VMEM((hops, 8, rows), full),
             pltpu.VMEM((hops, 8, rows), full),
             pltpu.VMEM((width, rank), half),

time: 184 us -> 185 us (level); the launches traced: 181 us -> 185 us
  Pallas kernels: 181 us -> 185 us
    pallas_call x1, Pallas kernels: 176 us -> 180 us  [body(): pl.pallas_call(functools.partial(relay_kernel, n_section, n_expert), out_...]
where the time goes in v7:
time: 185 us
  Pallas kernels  185 us (100%)
    pallas_call x1, Pallas kernels, body(): pl.pallas_call(functools.partial(relay_kernel, n_section, n_expert), out_...  180 us
    pallas_call x1, Pallas kernels, body(): pl.pallas_call(last_kernel, out_shape=jax.ShapeDtypeStruct((width, rows),...  4.87 us

profile of v7, /device:TPU:24, one launch (start us, length us, event | category | flops | bytes accessed | tf_op | source)
XLA Modules:
  0.0 184.7 jit_solution(7251370437181019514)
XLA Ops:
  0.0 179.8 %shard_map.82 = (bf16[2880,512]{1,0:T(8,128)(2,1)}, bf16[48,2880]{1,0:T(8,128)(2,1)}, f32[8,512]{1,0:T(8,128)}) custom-call(bf16[2880,512]{1,0:T(8,128)(2,1)} %bitcast.13, f32[1,2880]{1,0:T(1,128)} %gain_ref.1, s32[4,4,512]{2,1,0:T(4,128)} %bitcast.17, bf16[4,4,512]{2,1,0:T(4,128)(2,1)} %bitcast.18, bf16[2880,128]{1,0:T(8,128)(2,1)} %bitcast.15, ...), custom_call_target="tpu_custom_call" | custom-call | flops 7797473280 | bytes 16777216 | tf_op jit(solution)/shard_map/pallas_call | solution.py:536
  179.8 4.9 %shard_map.83 = bf16[2880,512]{1,0:T(8,128)(2,1)} custom-call(bf16[2880,512]{1,0:T(8,128)(2,1)} %get-tuple-element.8.adapted_ref, bf16[48,2880]{1,0:T(8,128)(2,1)} %get-tuple-element.9.expert_ref, f32[8,512]{1,0:T(8,128)} %get-tuple-element.10.meta_ref), custom_call_target="tpu_custom_call" | custom-call | flops 141557760 | bytes 5898240 | tf_op jit(solution)/shard_map/pallas_call | solution.py:617
